TPU v7x, 512 devices: a whole 4x8x8 slice. The times are simulated.
512 devices in a mesh: row: 128 (over y, x_hi, z), rep: 4 (over x_lo, core).
Axes of the slice: x: 4 (x_hi: 2, x_lo: 2; x = x_hi * 2 + x_lo), y: 8, z: 8, core: 2. Of those that a mesh axis runs over, the one named last changes fastest.
Arguments:
- features_t: bfloat16 [128, 32768], P('rep', 'row'), may hold values from -6 to 6
- tile_values: bfloat16 [16384, 128, 128], P('row'), may hold values from -0.09375 to 0.09375
- tile_rows: int32 [16384], P('row'), may hold values from 0 to 1, as said below
- tile_cols: int32 [16384], P('row'), may hold values from 0 to 255, as said below
- tile_count: int32 [128], P('row'), may hold values from 1 to 128, as said below
- weight: bfloat16 [128, 256], replicated, may hold values from -0.5 to 0.5
- cotangent: bfloat16 [32768, 256], P('row', 'rep'), may hold values from -0.078125 to 0.078125
Outputs:
- hidden: bfloat16 [32768, 256], P('row', 'rep')
- d_weight: float32 [128, 256], P('rep')
Inputs may be any that keep to these rules, and one draw needn't show every extreme that they name: `tile_rows`: within one node block all 128 slots name distinct (tile row, tile column) pairs; slots at or past the block's count are padding and carry no adjacency. `tile_cols`: tile column of each slot, distinct pairs with tile_rows within a block. Live slots of a block are its first tile_count slots; some block is full.
All inputs are finite; a program needn't handle non-finite values.
Results may differ from a plain program's by a relative error of at most 0.0054.
Values may be sent and summed in bfloat16 or wider, within the bound.
A program may use at most 64 MiB of HBM per device.

v0:
```python
import jax
import jax.numpy as jnp
from jax import lax
from jax.sharding import PartitionSpec as P


def tile_products(feature_table, tile_block, rows_here, cols_here, live_slots, tile_rows_dev):
    local_width = feature_table.shape[0]
    tile_size = tile_block.shape[1]
    grid = feature_table.reshape(local_width, -1, tile_size)
    picked = jnp.take(grid, cols_here, axis=1)
    terms = jnp.einsum("fsk,sdk->sfd", picked, tile_block, preferred_element_type=jnp.float32)
    row_select = (rows_here[:, None] == jnp.arange(tile_rows_dev, dtype=jnp.int32)[None, :]).astype(
        jnp.float32
    )
    row_select = row_select * live_slots.astype(jnp.float32)[:, None]
    summed = jnp.einsum("sfd,st->ftd", terms, row_select, precision=lax.Precision.HIGHEST)
    return summed.reshape(local_width, tile_rows_dev * tile_size)


def shards(features_t, tile_values, tile_rows, tile_cols, tile_count, weight, cotangent):
    slots = tile_values.shape[0]
    tile_size = tile_values.shape[1]
    tile_rows_dev = features_t.shape[1] // tile_size
    rep_size = lax.axis_size("rep")
    rep_index = lax.axis_index("rep")
    live_count = tile_count[0]
    live_slots = jnp.arange(slots, dtype=jnp.int32) < live_count
    feature_table = lax.all_gather(features_t, "row", axis=1, tiled=True)
    summed = tile_products(
        feature_table, tile_values, tile_rows, tile_cols, live_slots, tile_rows_dev
    )
    aggregated = summed.astype(jnp.bfloat16)
    hidden_width = weight.shape[1]
    cols_dev = hidden_width // rep_size
    contract_first = (((0,), (0,)), ((), ()))
    full_rows = lax.all_gather(aggregated, "rep", axis=0, tiled=True)
    weight_cols = lax.dynamic_slice_in_dim(weight, rep_index * cols_dev, cols_dev, 1)
    pre = lax.dot_general(
        full_rows, weight_cols, contract_first, preferred_element_type=jnp.float32
    )
    hidden = jax.nn.silu(pre).astype(jnp.bfloat16)
    sigmoid_part = jax.nn.sigmoid(pre)
    slope_term = sigmoid_part + pre * sigmoid_part * (1.0 - sigmoid_part)
    d_pre = (cotangent.astype(jnp.float32) * slope_term).astype(jnp.bfloat16)
    grads_all = lax.all_gather(d_pre, "rep", axis=1, tiled=True)
    local_grad = jnp.dot(aggregated, grads_all, preferred_element_type=jnp.float32)
    d_weight = lax.psum(local_grad, "row")
    return (hidden, d_weight)


def solution(mesh):
    placed = (
        P("rep", "row"),
        P("row", None, None),
        P("row"),
        P("row"),
        P("row"),
        P(),
        P("row", "rep"),
    )
    return jax.shard_map(
        shards,
        mesh=mesh,
        in_specs=placed,
        out_specs=(P("row", "rep"), P("rep", None)),
        check_vma=False,
    )
```

profile of v0, /device:TPU:2, one launch (start us, length us, event | category | flops | bytes accessed | tf_op | source)
XLA Modules:
  0.0 870.4 jit_solution(10839639451198216730)
XLA Ops:
  7.2 0.0 copy-start
  7.2 0.0 all-gather.2.cloned.1.call-start
  7.2 0.7 all-gather.2.cloned.1.call-update
  8.6 0.7 compare_select_fusion
  9.2 0.7 compare_and_fusion
  9.9 127.4 %all-gather.2.cloned.1.call-done = bf16[32,32768]{1,0:T(8,128)(2,1)} async-done(((bf16[32,256]{1,0:T(8,128)(2,1)}), bf16[32,32768]{1,0:T(8,128)(2,1)}) %all-gather.2.cloned.1.call-update) | async-done | bytes 2097168 | tf_op jit(solution)/shard_map/all_gather | solution.py:29
  137.3 2.0 copy_bitcast_fusion
  139.3 0.8 gather_fusion
  140.0 0.0 copy-start.1
  140.1 4.5 fusion.5
  144.6 0.0 copy-done.1
  144.6 0.0 copy-start.2
  144.6 2.2 fusion.2
  146.8 5.2 all_gather.10
  152.1 0.0 copy-done
  152.1 0.0 copy-done.2
  152.1 0.9 multiply_convert_fusion
  153.0 5.4 all_gather.11
  158.4 0.1 fusion.23
  158.5 705.1 %psum.7 = f32[32,256]{1,0:T(8,128)} all-reduce(f32[32,256]{1,0:T(8,128)S(1)} %fusion.23), channel_id=1, replica_groups=mesh['row'=128,'rep'=4] {'row'}, use_global_device_ids=true, to_apply=%region_0.1 | all-reduce | flops 8192 | bytes 65536 | tf_op jit(solution)/shard_map/psum | solution.py:48
  (3 shorter events, 0.0 us)
Async XLA Ops:
  7.2 144.9 %copy-start = (bf16[128,256]{1,0:T(8,128)(2,1)S(1)}, bf16[128,256]{1,0:T(8,128)(2,1)}, u32[]{:S(2)}) copy-start(bf16[128,256]{1,0:T(8,128)(2,1)} %param.12) | copy-start | bytes 196612
  7.2 130.1 %all-gather.2.cloned.1.call-start = ((), (), s32[]{:S(2)}) async-start(), calls=%async_computation | async-start | bytes 2113536 | tf_op jit(solution)/shard_map/all_gather | solution.py:29
  140.0 4.5 copy-start.1
  144.6 7.5 copy-start.2
Sparse Core Ops, SparseCore 0:
  12.1 125.1 all-gather.1
where the time goes:
time: 871 us; the launch traced here: 870 us
  blocking collectives  716 us (82%)
  waiting for transfers between devices  128 us (15%)
  between operations  14.7 us (2%)
    psum x1, blocking collectives, shards(): d_weight = lax.psum(local_grad, 'row')  705 us
    all_gather x1, waiting for transfers between devices, shards(): feature_table = lax.all_gather(features_t, 'row', axis=1, tiled=True)  127 us
  transfers between devices with their start and end apart: 1, of which 1 were waited for; matrix products, arithmetic and copies ran while one was open for 0% of the time, Pallas kernels for 0%

commit v1 on v0

v1 whole, which is shorter than its diff:
```python
import functools

import jax
import jax.numpy as jnp
from jax import lax
from jax.experimental import pallas as pl
from jax.experimental.pallas import tpu as pltpu
from jax.sharding import PartitionSpec as P

MESH = pl.DeviceIdType.MESH
NY, NX, NZ, NREP = 8, 2, 8, 4
RING = 8
GROUP = 16
SUB = 4
PER = GROUP // SUB
STEPS = (RING // 2 - 1) * SUB + SUB // 2
TILE = 128
SLOTS = 128
BATCH = 8


def kernel(
    rows_ref, cols_ref, count_ref, feat_ref, tv_hbm, weight_ref, cot_ref,
    hidden_ref, dw_ref,
    table, tv, index_s, own, cot_all, agg_all, w_t, rs_src, rs_buf, mid_src, mid_buf, end_buf,
    tv_sem, first_send, first_recv, ring_send, ring_recv,
    cot_send, cot_recv, agg_send, agg_recv,
    rs_send, rs_recv, mid_send, mid_recv, end_send, end_recv,
):
    row = lax.axis_index("row")
    rep = lax.axis_index("rep")
    y = row // (NX * NZ)
    xh = (row // NZ) % NX
    z = row % NZ

    def at(y_, x_, z_):
        return (y_ * NX + x_) * NZ + z_

    def y_peer(p):
        return at((y + p // NX) % NY, (xh + p % NX) % NX, z)

    def z_peer(p):
        return at(y, (xh + p % NX) % NX, (z + p // NX) % NZ)

    barrier = pltpu.get_barrier_semaphore()

    @pl.loop(1, GROUP)
    def _(p):
        pl.semaphore_signal(barrier, inc=1, device_id=(y_peer(p), rep), device_id_type=MESH)
        pl.semaphore_signal(barrier, inc=1, device_id=(z_peer(p), rep), device_id_type=MESH)

    @pl.loop(1, NREP)
    def _(p):
        pl.semaphore_signal(barrier, inc=1, device_id=(row, (rep + p) % NREP), device_id_type=MESH)

    load = pltpu.make_async_copy(tv_hbm, tv, tv_sem)
    load.start()
    own[0] = feat_ref[:, :TILE]
    own[1] = feat_ref[:, TILE:]
    g_y = y * NX + xh
    g_z = z * NX + xh
    place_a = z * GROUP + g_y
    place_b = RING * GROUP + y * GROUP + g_z
    pltpu.make_async_copy(own.at[0], table.at[place_a], first_recv.at[0, g_y // PER]).start()
    pltpu.make_async_copy(own.at[1], table.at[place_b], first_recv.at[1, g_z // PER]).start()
    cot_all[rep] = cot_ref[...]
    pl.semaphore_wait(barrier, 2 * (GROUP - 1) + NREP - 1)

    @pl.loop(1, GROUP)
    def _(p):
        pltpu.make_async_remote_copy(
            src_ref=own.at[0], dst_ref=table.at[place_a],
            send_sem=first_send.at[0], recv_sem=first_recv.at[0, g_y // PER],
            device_id=(y_peer(p), rep), device_id_type=MESH,
        ).start()
        pltpu.make_async_remote_copy(
            src_ref=own.at[1], dst_ref=table.at[place_b],
            send_sem=first_send.at[1], recv_sem=first_recv.at[1, g_z // PER],
            device_id=(z_peer(p), rep), device_id_type=MESH,
        ).start()

    @pl.loop(1, NREP)
    def _(p):
        pltpu.make_async_remote_copy(
            src_ref=cot_all.at[rep], dst_ref=cot_all.at[rep],
            send_sem=cot_send, recv_sem=cot_recv,
            device_id=(row, (rep + p) % NREP), device_id_type=MESH,
        ).start()

    w_t[...] = weight_ref[...].astype(jnp.float32).T.astype(jnp.bfloat16)

    @pl.loop(0, SLOTS)
    def _(s):
        col = cols_ref[s]
        odd = col % 2
        blk = col // 2
        by = blk // (NX * NZ)
        bx = (blk // NZ) % NX
        bz = blk % NZ
        place = jnp.where(
            odd == 0, bz * GROUP + by * NX + bx, RING * GROUP + by * GROUP + bz * NX + bx
        )
        index_s[s] = place

    def waits(ref, sem):
        pltpu.make_async_copy(ref, ref, sem).wait()

    def stream(k):
        half, side = k // 2, k % 2
        sign = 1 - 2 * side
        mine = z if half == 0 else y
        if half == 0:
            to = at(y, xh, (z + sign + NZ) % NZ)
        else:
            to = at((y + sign + NY) % NY, xh, z)
        return half, side, sign, mine, to

    def piece(k, i, shift):
        half, side, sign, mine, _ = stream(k)
        step = i // SUB
        q = i % SUB
        q = jnp.where(step == RING // 2 - 1, q + (SUB // 2) * side, q)
        grp = (mine - sign * (step + shift) + 2 * RING) % RING
        return table.at[pl.ds(half * RING * GROUP + grp * GROUP + q * PER, PER)]

    def send(k, i):
        to = stream(k)[4]
        ref = piece(k, i, 0)
        pltpu.make_async_remote_copy(
            src_ref=ref, dst_ref=ref,
            send_sem=ring_send.at[k], recv_sem=ring_recv.at[k, i],
            device_id=(to, rep), device_id_type=MESH,
        ).start()

    @pl.loop(0, SUB)
    def _(i):
        for half in range(2):
            waits(piece(2 * half, i, 0), first_recv.at[half, i])
            send(2 * half, i)
            send(2 * half + 1, i)

    last = SUB * (RING // 2 - 1)

    @pl.loop(SUB, last)
    def _(i):
        for k in range(4):
            waits(piece(k, i, 0), ring_recv.at[k, i - SUB])
            send(k, i)

    for i in range(last, last + SUB):
        for k in range(4):
            side = k % 2
            waits(piece(k, i - SUB, 1), ring_recv.at[k, i - SUB])
            j = i - (SUB // 2) * side
            if last <= j < STEPS:
                send(k, j)
    for i in range(last, STEPS):
        for k in range(4):
            waits(piece(k, i, 1), ring_recv.at[k, i])

    load.wait()
    count = count_ref[0]

    def batch(b, acc):
        picks = []
        for j in range(BATCH):
            s = b * BATCH + j
            tile = table[index_s[s]]
            live = s < count
            r = rows_ref[s]
            zero = jnp.zeros_like(tile)
            up = jnp.where(live & (r == 0), tile, zero)
            down = jnp.where(live & (r == 1), tile, zero)
            picks.append(jnp.concatenate([up, down], axis=0))
        lhs = jnp.concatenate(picks, axis=1)
        rhs = jnp.concatenate([tv[b * BATCH + j] for j in range(BATCH)], axis=1)
        return acc + lax.dot_general(
            lhs, rhs, (((1,), (1,)), ((), ())), preferred_element_type=jnp.float32
        )

    acc = lax.fori_loop(0, SLOTS // BATCH, batch, jnp.zeros((64, TILE), jnp.float32))
    agg = jnp.concatenate([acc[:32], acc[32:]], axis=1).astype(jnp.bfloat16)
    agg_all[rep] = agg

    @pl.loop(1, NREP)
    def _(p):
        pltpu.make_async_remote_copy(
            src_ref=agg_all.at[rep], dst_ref=agg_all.at[rep],
            send_sem=agg_send, recv_sem=agg_recv,
            device_id=(row, (rep + p) % NREP), device_id_type=MESH,
        ).start()

    three = pl.ds(0, NREP - 1)
    waits(cot_all.at[three], cot_recv)
    waits(agg_all.at[three], agg_recv)

    full = agg_all[...].reshape(4 * 32, 2 * TILE)
    pre_t = jnp.dot(w_t[...], full, preferred_element_type=jnp.float32)
    gate = jax.nn.sigmoid(pre_t)
    slope = gate + pre_t * gate * (1.0 - gate)
    cot = cot_all[...].reshape(4 * 64, 2 * TILE).astype(jnp.float32)
    d_pre_t = (cot * slope).astype(jnp.bfloat16)
    grad = lax.dot_general(
        agg, d_pre_t, (((1,), (1,)), ((), ())), preferred_element_type=jnp.float32
    )
    for j in range(8):
        rs_src[j] = grad[8 * (j // 2):8 * (j // 2) + 8, TILE * (j % 2):TILE * (j % 2) + TILE]
    rs_buf[y] = rs_src[y]

    @pl.loop(1, NY)
    def _(p):
        other = (y + p) % NY
        pltpu.make_async_remote_copy(
            src_ref=rs_src.at[other], dst_ref=rs_buf.at[y],
            send_sem=rs_send, recv_sem=rs_recv,
            device_id=(at(other, xh, z), rep), device_id_type=MESH,
        ).start()

    own_t = jnp.dot(
        w_t[pl.ds(pl.multiple_of(rep * 64, 64), 64), :], full, preferred_element_type=jnp.float32
    )
    hidden_t = own_t * jax.nn.sigmoid(own_t)
    hidden_ref[...] = hidden_t.astype(jnp.bfloat16)

    waits(rs_buf.at[pl.ds(0, NY - 1)], rs_recv)
    total = rs_buf[0]
    for j in range(1, NY):
        total = total + rs_buf[j]
    mid_src[...] = total
    mid_buf[g_z] = total

    @pl.loop(1, GROUP)
    def _(p):
        pltpu.make_async_remote_copy(
            src_ref=mid_src, dst_ref=mid_buf.at[g_z],
            send_sem=mid_send, recv_sem=mid_recv,
            device_id=(z_peer(p), rep), device_id_type=MESH,
        ).start()

    waits(mid_buf.at[pl.ds(0, GROUP - 1)], mid_recv)
    total = mid_buf[0]
    for j in range(1, GROUP):
        total = total + mid_buf[j]
    end_buf[y] = total

    @pl.loop(1, NY)
    def _(p):
        pltpu.make_async_remote_copy(
            src_ref=end_buf.at[y], dst_ref=end_buf.at[y],
            send_sem=end_send, recv_sem=end_recv,
            device_id=(at((y + p) % NY, xh, z), rep), device_id_type=MESH,
        ).start()

    waits(end_buf.at[pl.ds(0, NY - 1)], end_recv)
    for j in range(8):
        dw_ref[8 * (j // 2):8 * (j // 2) + 8, TILE * (j % 2):TILE * (j % 2) + TILE] = end_buf[j]

    for half in range(2):
        waits(table.at[pl.ds(0, GROUP - 1)], first_send.at[half])
    for k in range(4):
        waits(table.at[pl.ds(0, STEPS * PER)], ring_send.at[k])
    waits(cot_all.at[three], cot_send)
    waits(agg_all.at[three], agg_send)
    waits(rs_buf.at[pl.ds(0, NY - 1)], rs_send)
    waits(mid_buf.at[pl.ds(0, GROUP - 1)], mid_send)
    waits(end_buf.at[pl.ds(0, NY - 1)], end_send)


def shards(features_t, tile_values, tile_rows, tile_cols, tile_count, weight, cotangent):
    vmem = pl.BlockSpec(memory_space=pltpu.VMEM)
    smem = pl.BlockSpec(memory_space=pltpu.SMEM)
    dma = pltpu.SemaphoreType.DMA
    bf16, f32 = jnp.bfloat16, jnp.float32
    hidden_t, d_weight = pl.pallas_call(
        kernel,
        out_shape=(
            jax.ShapeDtypeStruct((64, 256), bf16),
            jax.ShapeDtypeStruct((32, 256), f32),
        ),
        in_specs=[smem, smem, smem, vmem, pl.BlockSpec(memory_space=pl.ANY), vmem, vmem],
        out_specs=(vmem, vmem),
        scratch_shapes=[
            pltpu.VMEM((2 * RING * GROUP, 32, TILE), bf16),
            pltpu.VMEM((SLOTS, TILE, TILE), bf16),
            pltpu.SMEM((SLOTS,), jnp.int32),
            pltpu.VMEM((2, 32, TILE), bf16),
            pltpu.VMEM((NREP, 64, 256), bf16),
            pltpu.VMEM((NREP, 32, 256), bf16),
            pltpu.VMEM((256, 128), bf16),
            pltpu.VMEM((8, 8, TILE), f32),
            pltpu.VMEM((8, 8, TILE), f32),
            pltpu.VMEM((8, TILE), f32),
            pltpu.VMEM((GROUP, 8, TILE), f32),
            pltpu.VMEM((8, 8, TILE), f32),
            dma(()), dma((2,)), dma((2, SUB)), dma((4,)), dma((4, STEPS)),
            dma(()), dma(()), dma(()), dma(()),
            dma(()), dma(()), dma(()), dma(()), dma(()), dma(()),
        ],
        compiler_params=pltpu.CompilerParams(
            collective_id=0, has_side_effects=True, vmem_limit_bytes=56 * 1024 * 1024
        ),
        name="layer",
    )(tile_rows, tile_cols, tile_count, features_t, tile_values, weight, cotangent.T)
    return hidden_t.T, d_weight


def solution(mesh):
    placed = (
        P("rep", "row"),
        P("row", None, None),
        P("row"),
        P("row"),
        P("row"),
        P(),
        P("row", "rep"),
    )
    return jax.shard_map(
        shards,
        mesh=mesh,
        in_specs=placed,
        out_specs=(P("row", "rep"), P("rep", None)),
        check_vma=False,
    )
```

time: 871 us -> 66.3 us (0.08)
  the two profiles are of different devices: /device:TPU:2 before, /device:TPU:16 now
where the time goes in v1:
time: 66.3 us; the launch traced here: 66 us
  Pallas kernels  61.9 us (93%)
  local copies, waits for them, and re-layouts  2.75 us (4%)
  between operations  1.29 us (2%)
    pallas_call x1, Pallas kernels, shards(): pl.pallas_call(kernel, out_shape=(jax.ShapeDtypeStruct((64, 256), bf16),...  61.9 us
    unnamed x2, local copies, waits for them, and re-layouts  2.75 us

profile of v1, /device:TPU:16, one launch (start us, length us, event | category | flops | bytes accessed | tf_op | source)
XLA Modules:
  0.0 66.0 jit_solution(324374833352740883)
XLA Ops:
  1.3 61.9 %layer.1 = (bf16[64,256]{1,0:T(8,128)(2,1)}, f32[32,256]{1,0:T(8,128)}) custom-call(s32[128]{0:T(128)} %rows_ref.1, s32[128]{0:T(128)} %cols_ref.1, s32[1]{0:T(128)S(6)} %copy.11.count_ref, bf16[32,256]{1,0:T(8,128)(2,1)} %feat_ref.1, bf16[128,128,128]{2,1,0:T(8,128)(2,1)} %tv_hbm.1, bf16[128,256]{1,0:T(8,128)(2,1)} %weight_ref.1, bf16[64,256]{1,0:T(8,128)(2,1)} %bitcast.2), custom_call_target="tpu_custom_call" | custom-call | tf_op jit(solution)/shard_map/layer/pallas_call | solution.py:274
  63.2 1.4 %copy.12 = bf16[256,64]{0,1:T(8,128)(2,1)} copy(bf16[256,64]{0,1:T(8,128)(2,1)} %bitcast.3) | data formatting | bytes 65536
  64.6 1.4 %copy.13 = f32[32,256]{1,0:T(8,128)} copy(f32[32,256]{1,0:T(8,128)} %get-tuple-element.9) | data formatting | bytes 65536

commit v2 on v1

v2 whole, which is shorter than its diff:
```python
import jax
import jax.numpy as jnp
from jax import lax
from jax.experimental import pallas as pl
from jax.experimental.pallas import tpu as pltpu
from jax.sharding import PartitionSpec as P

MESH = pl.DeviceIdType.MESH
NY, NX, NZ, NREP = 8, 2, 8, 4
RING = 8
GROUP = 16
SUB = 8
PER = GROUP // SUB
STEPS = (RING // 2 - 1) * SUB + SUB // 2
TILE = 128
SLOTS = 128
BATCH = 8


def rank(d):
    return jnp.where(d == 0, 0, jnp.where(d <= RING // 2, 2 * d - 1, 2 * (RING - d)))


def far_first(k):
    return RING // 2 + ((k + 1) // 2) * (1 - 2 * (k % 2))


def kernel(
    rows_hbm, cols_hbm, count_hbm, feat_hbm, tv_hbm, weight_hbm, cot_hbm,
    hidden_ref, dw_ref,
    rows_ref, cols_ref, count_ref, index_s, code_s,
    table, tv, weight, cot_all, agg_all, w_t, rs_src, rs_buf, mid_src, mid_buf, end_buf,
    tv_sem, in_sem, x_send, first_send, first_recv, ring_send, ring_recv,
    cot_send, cot_recv, agg_send, agg_recv,
    rs_send, rs_recv, mid_send, mid_recv, end_send, end_recv,
):
    row = lax.axis_index("row")
    rep = lax.axis_index("rep")
    y = row // (NX * NZ)
    xh = (row // NZ) % NX
    z = row % NZ

    def at(y_, x_, z_):
        return (y_ * NX + x_) * NZ + z_

    def y_peer(d):
        return at((y + d) % NY, xh, z)

    def z_peer(d):
        return at(y, xh, (z + d) % NZ)

    def peer(half, d):
        return y_peer(d) if half == 0 else z_peer(d)

    other_x = at(y, 1 - xh, z)

    def waits(ref, sem):
        pltpu.make_async_copy(ref, ref, sem).wait()

    def put(src, dst, send_sem, recv_sem, to, rep_to=None):
        pltpu.make_async_remote_copy(
            src_ref=src, dst_ref=dst, send_sem=send_sem, recv_sem=recv_sem,
            device_id=(to, rep if rep_to is None else rep_to), device_id_type=MESH,
        ).start()

    barrier = pltpu.get_barrier_semaphore()

    def greet(to, rep_to):
        pl.semaphore_signal(barrier, inc=1, device_id=(to, rep_to), device_id_type=MESH)

    @pl.loop(0, RING - 1)
    def _(k):
        greet(y_peer(far_first(k)), rep)
        greet(z_peer(far_first(k)), rep)

    greet(other_x, rep)

    @pl.loop(1, NREP)
    def _(p):
        greet(row, (rep + p) % NREP)

    base = (z * GROUP, RING * GROUP + y * GROUP)
    ins = [
        pltpu.make_async_copy(feat_hbm.at[:, pl.ds(0, TILE)], table.at[base[0]], in_sem.at[0]),
        pltpu.make_async_copy(feat_hbm.at[:, pl.ds(TILE, TILE)], table.at[base[1]], in_sem.at[1]),
        pltpu.make_async_copy(cot_hbm, cot_all.at[rep], in_sem.at[2]),
        pltpu.make_async_copy(weight_hbm, weight, in_sem.at[3]),
        pltpu.make_async_copy(rows_hbm, rows_ref, in_sem.at[4]),
        pltpu.make_async_copy(cols_hbm, cols_ref, in_sem.at[5]),
        pltpu.make_async_copy(count_hbm, count_ref, in_sem.at[6]),
    ]
    for c in ins:
        c.start()
    load = pltpu.make_async_copy(tv_hbm, tv, tv_sem)
    load.start()
    ins[0].wait()
    ins[1].wait()
    pl.semaphore_wait(barrier, 2 * (RING - 1) + 1 + NREP - 1)

    for half in range(2):
        put(table.at[base[half]], table.at[base[half] + 1], x_send.at[half],
            first_recv.at[half, 0], other_x)

    def spread(j, sem):
        @pl.loop(0, RING - 1)
        def _(k):
            d = far_first(k)
            r = rank(RING - d)
            for half in range(2):
                put(table.at[base[half] + j], table.at[base[half] + 2 * r + j],
                    first_send.at[half], first_recv.at[half, r], peer(half, d))

    spread(0, 0)
    ins[2].wait()

    @pl.loop(1, NREP)
    def _(p):
        put(cot_all.at[rep], cot_all.at[rep], cot_send, cot_recv, row, (rep + p) % NREP)

    for half in range(2):
        waits(table.at[0], first_recv.at[half, 0])
    spread(1, 1)

    def piece(k, i, shift):
        half, side = k // 2, k % 2
        sign = 1 - 2 * side
        mine = z if half == 0 else y
        step = i // SUB
        q = i % SUB
        q = jnp.where(step == RING // 2 - 1, q + (SUB // 2) * side, q)
        grp = (mine - sign * (step + shift) + 2 * RING) % RING
        return table.at[pl.ds(half * RING * GROUP + grp * GROUP + q * PER, PER)]

    def send(k, i):
        half, sign = k // 2, 1 - 2 * (k % 2)
        ref = piece(k, i, 0)
        put(ref, ref, ring_send.at[k], ring_recv.at[k, i], peer(1 - half, sign + RING))

    for k in range(4):
        send(k, 0)

    @pl.loop(1, SUB)
    def _(i):
        for half in range(2):
            waits(piece(2 * half, i, 0), first_recv.at[half, i])
            send(2 * half, i)
            send(2 * half + 1, i)

    last = SUB * (RING // 2 - 1)

    @pl.loop(SUB, last)
    def _(i):
        for k in range(4):
            waits(piece(k, i, 0), ring_recv.at[k, i - SUB])
            send(k, i)

    @pl.loop(last, STEPS)
    def _(i):
        for k in (0, 2):
            waits(piece(k, i - SUB, 1), ring_recv.at[k, i - SUB])
            send(k, i)
        for k in (1, 3):
            waits(piece(k, i - SUB, 1), ring_recv.at[k, i - SUB])

    @pl.loop(last, STEPS)
    def _(i):
        for k in (0, 2):
            waits(piece(k, i - SUB // 2, 1), ring_recv.at[k, i - SUB // 2])
        for k in (1, 3):
            waits(piece(k, i - SUB // 2, 1), ring_recv.at[k, i - SUB // 2])
            send(k, i)

    for c in ins[3:]:
        c.wait()
    w_t[...] = weight[...].astype(jnp.float32).T.astype(jnp.bfloat16)
    count = count_ref[0]

    @pl.loop(0, SLOTS)
    def _(s):
        col = cols_ref[s]
        blk = col // 2
        by = blk // (NX * NZ)
        dx = ((blk // NZ) + xh) % NX
        bz = blk % NZ
        place_a = bz * GROUP + rank((by - y + NY) % NY) * 2 + dx
        place_b = RING * GROUP + by * GROUP + rank((bz - z + NZ) % NZ) * 2 + dx
        index_s[s] = jnp.where(col % 2 == 0, place_a, place_b)
        code_s[s] = jnp.where(s < count, rows_ref[s], 2)

    @pl.loop(last, STEPS)
    def _(i):
        for k in range(4):
            waits(piece(k, i, 1), ring_recv.at[k, i])

    load.wait()

    def batch(b, acc):
        picks = []
        for j in range(BATCH):
            s = b * BATCH + j
            tile = table[index_s[s]]
            r = code_s[s]
            zero = jnp.zeros_like(tile)
            up = jnp.where(r == 0, tile, zero)
            down = jnp.where(r == 1, tile, zero)
            picks.append(jnp.concatenate([up, down], axis=0))
        lhs = jnp.concatenate(picks, axis=1)
        rhs = jnp.concatenate([tv[b * BATCH + j] for j in range(BATCH)], axis=1)
        return acc + lax.dot_general(
            lhs, rhs, (((1,), (1,)), ((), ())), preferred_element_type=jnp.float32
        )

    acc = lax.fori_loop(0, SLOTS // BATCH, batch, jnp.zeros((64, TILE), jnp.float32))
    agg = jnp.concatenate([acc[:32], acc[32:]], axis=1).astype(jnp.bfloat16)
    agg_all[rep] = agg

    @pl.loop(1, NREP)
    def _(p):
        put(agg_all.at[rep], agg_all.at[rep], agg_send, agg_recv, row, (rep + p) % NREP)

    three = pl.ds(0, NREP - 1)
    waits(cot_all.at[three], cot_recv)
    waits(agg_all.at[three], agg_recv)

    full = agg_all[...].reshape(4 * 32, 2 * TILE)
    pre_t = jnp.dot(w_t[...], full, preferred_element_type=jnp.float32)
    gate = jax.nn.sigmoid(pre_t)
    slope = gate + pre_t * gate * (1.0 - gate)
    cot = cot_all[...].reshape(4 * 64, 2 * TILE).astype(jnp.float32)
    d_pre_t = (cot * slope).astype(jnp.bfloat16)
    grad = lax.dot_general(
        agg, d_pre_t, (((1,), (1,)), ((), ())), preferred_element_type=jnp.float32
    )
    for j in range(8):
        rs_src[j] = grad[8 * (j // 2):8 * (j // 2) + 8, TILE * (j % 2):TILE * (j % 2) + TILE]

    @pl.loop(0, NY - 1)
    def _(k):
        other = (y + far_first(k)) % NY
        put(rs_src.at[other], rs_buf.at[y], rs_send, rs_recv, at(other, xh, z))

    rs_buf[y] = rs_src[y]

    own_t = jnp.dot(
        w_t[pl.ds(pl.multiple_of(rep * 64, 64), 64), :], full, preferred_element_type=jnp.float32
    )
    hidden_ref[...] = (own_t * jax.nn.sigmoid(own_t)).astype(jnp.bfloat16)

    seven = pl.ds(0, RING - 1)
    waits(rs_buf.at[seven], rs_recv)
    total = rs_buf[0]
    for j in range(1, NY):
        total = total + rs_buf[j]
    mid_src[...] = total
    g_z = z * NX + xh

    @pl.loop(0, RING - 1)
    def _(k):
        z_to = (z + far_first(k)) % NZ
        put(mid_src, mid_buf.at[g_z], mid_send, mid_recv, at(y, 1 - xh, z_to))
        put(mid_src, mid_buf.at[g_z], mid_send, mid_recv, at(y, xh, z_to))

    put(mid_src, mid_buf.at[g_z], mid_send, mid_recv, other_x)
    mid_buf[g_z] = total

    fifteen = pl.ds(0, GROUP - 1)
    waits(mid_buf.at[fifteen], mid_recv)
    total = mid_buf[0]
    for j in range(1, GROUP):
        total = total + mid_buf[j]
    end_buf[y] = total

    @pl.loop(0, RING - 1)
    def _(k):
        put(end_buf.at[y], end_buf.at[y], end_send, end_recv, y_peer(far_first(k)))

    waits(end_buf.at[seven], end_recv)
    for j in range(8):
        dw_ref[8 * (j // 2):8 * (j // 2) + 8, TILE * (j % 2):TILE * (j % 2) + TILE] = end_buf[j]

    for half in range(2):
        waits(table.at[0], x_send.at[half])
        waits(table.at[pl.ds(0, 2 * (RING - 1))], first_send.at[half])
    for k in range(4):
        waits(table.at[pl.ds(0, STEPS * PER)], ring_send.at[k])
    waits(cot_all.at[three], cot_send)
    waits(agg_all.at[three], agg_send)
    waits(rs_buf.at[seven], rs_send)
    waits(mid_buf.at[fifteen], mid_send)
    waits(end_buf.at[seven], end_send)


def shards(features_t, tile_values, tile_rows, tile_cols, tile_count, weight, cotangent):
    vmem = pl.BlockSpec(memory_space=pltpu.VMEM)
    hbm = pl.BlockSpec(memory_space=pl.ANY)
    dma = pltpu.SemaphoreType.DMA
    bf16, f32 = jnp.bfloat16, jnp.float32
    hidden_t, d_weight = pl.pallas_call(
        kernel,
        out_shape=(
            jax.ShapeDtypeStruct((64, 256), bf16),
            jax.ShapeDtypeStruct((32, 256), f32),
        ),
        in_specs=[hbm] * 7,
        out_specs=(vmem, vmem),
        scratch_shapes=[
            pltpu.SMEM((SLOTS,), jnp.int32),
            pltpu.SMEM((SLOTS,), jnp.int32),
            pltpu.SMEM((1,), jnp.int32),
            pltpu.SMEM((SLOTS,), jnp.int32),
            pltpu.SMEM((SLOTS,), jnp.int32),
            pltpu.VMEM((2 * RING * GROUP, 32, TILE), bf16),
            pltpu.VMEM((SLOTS, TILE, TILE), bf16),
            pltpu.VMEM((128, 256), bf16),
            pltpu.VMEM((NREP, 64, 256), bf16),
            pltpu.VMEM((NREP, 32, 256), bf16),
            pltpu.VMEM((256, 128), bf16),
            pltpu.VMEM((8, 8, TILE), f32),
            pltpu.VMEM((8, 8, TILE), f32),
            pltpu.VMEM((8, TILE), f32),
            pltpu.VMEM((GROUP, 8, TILE), f32),
            pltpu.VMEM((8, 8, TILE), f32),
            dma(()), dma((7,)), dma((2,)), dma((2,)), dma((2, SUB)), dma((4,)), dma((4, STEPS)),
            dma(()), dma(()), dma(()), dma(()),
            dma(()), dma(()), dma(()), dma(()), dma(()), dma(()),
        ],
        compiler_params=pltpu.CompilerParams(
            collective_id=0, has_side_effects=True, vmem_limit_bytes=56 * 1024 * 1024
        ),
        name="layer",
    )(tile_rows, tile_cols, tile_count, features_t, tile_values, weight, cotangent.T)
    return hidden_t.T, d_weight


def solution(mesh):
    placed = (
        P("rep", "row"),
        P("row", None, None),
        P("row"),
        P("row"),
        P("row"),
        P(),
        P("row", "rep"),
    )
    return jax.shard_map(
        shards,
        mesh=mesh,
        in_specs=placed,
        out_specs=(P("row", "rep"), P("rep", None)),
        check_vma=False,
    )
```

time: 66.3 us -> 66.2 us (level)
  the two profiles are of different devices: /device:TPU:16 before, /device:TPU:8 now
where the time goes in v2:
time: 66.2 us; the launch traced here: 66 us
  Pallas kernels  61.9 us (94%)
  local copies, waits for them, and re-layouts  2.75 us (4%)
  between operations  1.29 us (2%)
    pallas_call x1, Pallas kernels, shards(): pl.pallas_call(kernel, out_shape=(jax.ShapeDtypeStruct((64, 256), bf16),...  61.9 us
    unnamed x2, local copies, waits for them, and re-layouts  2.75 us

profile of v2, /device:TPU:8, one launch (start us, length us, event | category | flops | bytes accessed | tf_op | source)
XLA Modules:
  0.0 66.0 jit_solution(10048272998785172498)
XLA Ops:
  1.3 61.9 %layer.1 = (bf16[64,256]{1,0:T(8,128)(2,1)}, f32[32,256]{1,0:T(8,128)}) custom-call(s32[128]{0:T(128)} %rows_hbm.1, s32[128]{0:T(128)} %cols_hbm.1, s32[1]{0:T(128)S(6)} %copy.11.count_hbm, bf16[32,256]{1,0:T(8,128)(2,1)} %feat_hbm.1, bf16[128,128,128]{2,1,0:T(8,128)(2,1)} %tv_hbm.1, bf16[128,256]{1,0:T(8,128)(2,1)} %weight_hbm.1, bf16[64,256]{1,0:T(8,128)(2,1)} %bitcast.2), custom_call_target="tpu_custom_call" | custom-call | tf_op jit(solution)/shard_map/layer/pallas_call | solution.py:298
  63.2 1.4 %copy.12 = bf16[256,64]{0,1:T(8,128)(2,1)} copy(bf16[256,64]{0,1:T(8,128)(2,1)} %bitcast.3) | data formatting | bytes 65536
  64.6 1.4 %copy.13 = f32[32,256]{1,0:T(8,128)} copy(f32[32,256]{1,0:T(8,128)} %get-tuple-element.9) | data formatting | bytes 65536

commit v3 on v2

--- a/solution.py
+++ b/solution.py
@@ -10,19 +10,23 @@
 RING = 8
 GROUP = 16
 SUB = 8
+LEAD = 5
 PER = GROUP // SUB
-STEPS = (RING // 2 - 1) * SUB + SUB // 2
 TILE = 128
 SLOTS = 128
 BATCH = 8
 
 
+def mod(a, n):
+    return lax.rem(a, jnp.int32(n))
+
+
 def rank(d):
     return jnp.where(d == 0, 0, jnp.where(d <= RING // 2, 2 * d - 1, 2 * (RING - d)))
 
 
 def far_first(k):
-    return RING // 2 + ((k + 1) // 2) * (1 - 2 * (k % 2))
+    return RING // 2 + lax.div(k + 1, jnp.int32(2)) * (1 - 2 * mod(k, 2))
 
 
 def kernel(
@@ -30,29 +34,22 @@
     hidden_ref, dw_ref,
     rows_ref, cols_ref, count_ref, index_s, code_s,
     table, tv, weight, cot_all, agg_all, w_t, rs_src, rs_buf, mid_src, mid_buf, end_buf,
-    tv_sem, in_sem, x_send, first_send, first_recv, ring_send, ring_recv,
+    tv_sem, in_sem, first_send, first_recv, ring_send, two_recv, rest_recv,
     cot_send, cot_recv, agg_send, agg_recv,
     rs_send, rs_recv, mid_send, mid_recv, end_send, end_recv,
 ):
     row = lax.axis_index("row")
     rep = lax.axis_index("rep")
-    y = row // (NX * NZ)
-    xh = (row // NZ) % NX
-    z = row % NZ
+    y = lax.div(row, jnp.int32(NX * NZ))
+    xh = mod(lax.div(row, jnp.int32(NZ)), NX)
+    z = mod(row, NZ)
 
     def at(y_, x_, z_):
         return (y_ * NX + x_) * NZ + z_
 
-    def y_peer(d):
-        return at((y + d) % NY, xh, z)
-
-    def z_peer(d):
-        return at(y, xh, (z + d) % NZ)
-
-    def peer(half, d):
-        return y_peer(d) if half == 0 else z_peer(d)
-
-    other_x = at(y, 1 - xh, z)
+    def peer(half, d, dx=0):
+        x_ = mod(xh + dx, NX)
+        return at(mod(y + d, NY), x_, z) if half == 0 else at(y, x_, mod(z + d, NZ))
 
     def waits(ref, sem):
         pltpu.make_async_copy(ref, ref, sem).wait()
@@ -70,14 +67,17 @@
 
     @pl.loop(0, RING - 1)
     def _(k):
-        greet(y_peer(far_first(k)), rep)
-        greet(z_peer(far_first(k)), rep)
-
-    greet(other_x, rep)
+        d = far_first(k)
+        for half in range(2):
+            greet(peer(half, d, 1), rep)
+            greet(peer(half, d), rep)
+
+    for half in range(2):
+        greet(peer(half, 0, 1), rep)
 
     @pl.loop(1, NREP)
     def _(p):
-        greet(row, (rep + p) % NREP)
+        greet(row, mod(rep + p, NREP))
 
     base = (z * GROUP, RING * GROUP + y * GROUP)
     ins = [
@@ -95,80 +95,75 @@
     load.start()
     ins[0].wait()
     ins[1].wait()
-    pl.semaphore_wait(barrier, 2 * (RING - 1) + 1 + NREP - 1)
+    pl.semaphore_wait(barrier, 2 * (GROUP - 1) + NREP - 1)
+
+    def spread(half, d, dx):
+        r = rank(mod(RING - d, RING))
+        put(table.at[base[half]], table.at[base[half] + 2 * r + dx],
+            first_send.at[half], first_recv.at[half, r], peer(half, d, dx))
 
     for half in range(2):
-        put(table.at[base[half]], table.at[base[half] + 1], x_send.at[half],
-            first_recv.at[half, 0], other_x)
-
-    def spread(j, sem):
-        @pl.loop(0, RING - 1)
-        def _(k):
-            d = far_first(k)
-            r = rank(RING - d)
-            for half in range(2):
-                put(table.at[base[half] + j], table.at[base[half] + 2 * r + j],
-                    first_send.at[half], first_recv.at[half, r], peer(half, d))
-
-    spread(0, 0)
+        spread(half, jnp.int32(0), 1)
+
+    @pl.loop(0, RING - 1)
+    def _(k):
+        for half in range(2):
+            spread(half, far_first(k), 1)
+            spread(half, far_first(k), 0)
+
     ins[2].wait()
 
     @pl.loop(1, NREP)
     def _(p):
-        put(cot_all.at[rep], cot_all.at[rep], cot_send, cot_recv, row, (rep + p) % NREP)
-
-    for half in range(2):
-        waits(table.at[0], first_recv.at[half, 0])
-    spread(1, 1)
-
-    def piece(k, i, shift):
-        half, side = k // 2, k % 2
-        sign = 1 - 2 * side
-        mine = z if half == 0 else y
-        step = i // SUB
-        q = i % SUB
-        q = jnp.where(step == RING // 2 - 1, q + (SUB // 2) * side, q)
-        grp = (mine - sign * (step + shift) + 2 * RING) % RING
-        return table.at[pl.ds(half * RING * GROUP + grp * GROUP + q * PER, PER)]
-
-    def send(k, i):
-        half, sign = k // 2, 1 - 2 * (k % 2)
-        ref = piece(k, i, 0)
-        put(ref, ref, ring_send.at[k], ring_recv.at[k, i], peer(1 - half, sign + RING))
-
-    for k in range(4):
-        send(k, 0)
-
-    @pl.loop(1, SUB)
-    def _(i):
-        for half in range(2):
-            waits(piece(2 * half, i, 0), first_recv.at[half, i])
-            send(2 * half, i)
-            send(2 * half + 1, i)
-
-    last = SUB * (RING // 2 - 1)
-
-    @pl.loop(SUB, last)
-    def _(i):
-        for k in range(4):
-            waits(piece(k, i, 0), ring_recv.at[k, i - SUB])
-            send(k, i)
-
-    @pl.loop(last, STEPS)
-    def _(i):
-        for k in (0, 2):
-            waits(piece(k, i - SUB, 1), ring_recv.at[k, i - SUB])
-            send(k, i)
-        for k in (1, 3):
-            waits(piece(k, i - SUB, 1), ring_recv.at[k, i - SUB])
-
-    @pl.loop(last, STEPS)
-    def _(i):
-        for k in (0, 2):
-            waits(piece(k, i - SUB // 2, 1), ring_recv.at[k, i - SUB // 2])
-        for k in (1, 3):
-            waits(piece(k, i - SUB // 2, 1), ring_recv.at[k, i - SUB // 2])
-            send(k, i)
+        put(cot_all.at[rep], cot_all.at[rep], cot_send, cot_recv, row, mod(rep + p, NREP))
+
+    mine = (z, y)
+    ahead = [
+        [[peer(1 - half, RING + sign * d) for d in (1, 2)] for sign in (1, -1)]
+        for half in range(2)
+    ]
+    from_two = [[mod(mine[half] + RING - 2 * sign, RING) for sign in (1, -1)] for half in range(2)]
+
+    def piece(half, grp, q, n=PER):
+        return table.at[pl.ds(half * RING * GROUP + grp * GROUP + q * PER, n)]
+
+    def own_piece(q, n=PER):
+        for half in range(2):
+            waits(piece(half, mine[half], q, n), first_recv.at[half, q])
+            ref = piece(half, mine[half], q)
+            for side in range(2):
+                put(ref, ref, ring_send.at[half, side], two_recv.at[half, side, q],
+                    ahead[half][side][1])
+                put(ref, ref, ring_send.at[half, side], rest_recv.at[half, side, 0],
+                    ahead[half][side][0])
+
+    def pass_piece(q):
+        for half in range(2):
+            for side in range(2):
+                ref = piece(half, from_two[half][side], q)
+                waits(ref, two_recv.at[half, side, q])
+                put(ref, ref, ring_send.at[half, side], rest_recv.at[half, side, 1],
+                    ahead[half][side][0])
+
+                @pl.when(mod(q, 2) == side)
+                def _():
+                    put(ref, ref, ring_send.at[half, side], rest_recv.at[half, side, 2],
+                        ahead[half][side][1])
+
+    own_piece(0, 1)
+
+    @pl.loop(1, LEAD)
+    def _(q):
+        own_piece(q)
+
+    @pl.loop(LEAD, SUB)
+    def _(q):
+        own_piece(q)
+        pass_piece(q - LEAD)
+
+    @pl.loop(SUB - LEAD, SUB)
+    def _(q):
+        pass_piece(q)
 
     for c in ins[3:]:
         c.wait()
@@ -178,19 +173,20 @@
     @pl.loop(0, SLOTS)
     def _(s):
         col = cols_ref[s]
-        blk = col // 2
-        by = blk // (NX * NZ)
-        dx = ((blk // NZ) + xh) % NX
-        bz = blk % NZ
-        place_a = bz * GROUP + rank((by - y + NY) % NY) * 2 + dx
-        place_b = RING * GROUP + by * GROUP + rank((bz - z + NZ) % NZ) * 2 + dx
-        index_s[s] = jnp.where(col % 2 == 0, place_a, place_b)
+        blk = lax.div(col, jnp.int32(2))
+        by = lax.div(blk, jnp.int32(NX * NZ))
+        dx = mod(lax.div(blk, jnp.int32(NZ)) + xh, NX)
+        bz = mod(blk, NZ)
+        place_a = bz * GROUP + rank(mod(by - y + NY, NY)) * 2 + dx
+        place_b = RING * GROUP + by * GROUP + rank(mod(bz - z + NZ, NZ)) * 2 + dx
+        index_s[s] = jnp.where(mod(col, 2) == 0, place_a, place_b)
         code_s[s] = jnp.where(s < count, rows_ref[s], 2)
 
-    @pl.loop(last, STEPS)
-    def _(i):
-        for k in range(4):
-            waits(piece(k, i, 1), ring_recv.at[k, i])
+    for kind in range(3):
+        for half in range(2):
+            for side in range(2):
+                waits(table.at[pl.ds(0, (GROUP, GROUP, GROUP // 2)[kind])],
+                      rest_recv.at[half, side, kind])
 
     load.wait()
 
@@ -216,7 +212,7 @@
 
     @pl.loop(1, NREP)
     def _(p):
-        put(agg_all.at[rep], agg_all.at[rep], agg_send, agg_recv, row, (rep + p) % NREP)
+        put(agg_all.at[rep], agg_all.at[rep], agg_send, agg_recv, row, mod(rep + p, NREP))
 
     three = pl.ds(0, NREP - 1)
     waits(cot_all.at[three], cot_recv)
@@ -236,7 +232,7 @@
 
     @pl.loop(0, NY - 1)
     def _(k):
-        other = (y + far_first(k)) % NY
+        other = mod(y + far_first(k), NY)
         put(rs_src.at[other], rs_buf.at[y], rs_send, rs_recv, at(other, xh, z))
 
     rs_buf[y] = rs_src[y]
@@ -256,11 +252,11 @@
 
     @pl.loop(0, RING - 1)
     def _(k):
-        z_to = (z + far_first(k)) % NZ
+        z_to = mod(z + far_first(k), NZ)
         put(mid_src, mid_buf.at[g_z], mid_send, mid_recv, at(y, 1 - xh, z_to))
         put(mid_src, mid_buf.at[g_z], mid_send, mid_recv, at(y, xh, z_to))
 
-    put(mid_src, mid_buf.at[g_z], mid_send, mid_recv, other_x)
+    put(mid_src, mid_buf.at[g_z], mid_send, mid_recv, at(y, 1 - xh, z))
     mid_buf[g_z] = total
 
     fifteen = pl.ds(0, GROUP - 1)
@@ -272,17 +268,16 @@
 
     @pl.loop(0, RING - 1)
     def _(k):
-        put(end_buf.at[y], end_buf.at[y], end_send, end_recv, y_peer(far_first(k)))
+        put(end_buf.at[y], end_buf.at[y], end_send, end_recv, peer(0, far_first(k)))
 
     waits(end_buf.at[seven], end_recv)
     for j in range(8):
         dw_ref[8 * (j // 2):8 * (j // 2) + 8, TILE * (j % 2):TILE * (j % 2) + TILE] = end_buf[j]
 
     for half in range(2):
-        waits(table.at[0], x_send.at[half])
-        waits(table.at[pl.ds(0, 2 * (RING - 1))], first_send.at[half])
-    for k in range(4):
-        waits(table.at[pl.ds(0, STEPS * PER)], ring_send.at[k])
+        waits(table.at[pl.ds(0, GROUP - 1)], first_send.at[half])
+        for side in range(2):
+            waits(table.at[pl.ds(0, 7 * GROUP // 2)], ring_send.at[half, side])
     waits(cot_all.at[three], cot_send)
     waits(agg_all.at[three], agg_send)
     waits(rs_buf.at[seven], rs_send)
@@ -320,7 +315,8 @@
             pltpu.VMEM((8, TILE), f32),
             pltpu.VMEM((GROUP, 8, TILE), f32),
             pltpu.VMEM((8, 8, TILE), f32),
-            dma(()), dma((7,)), dma((2,)), dma((2,)), dma((2, SUB)), dma((4,)), dma((4, STEPS)),
+            dma(()), dma((7,)), dma((2,)), dma((2, SUB)),
+            dma((2, 2)), dma((2, 2, SUB)), dma((2, 2, 3)),
             dma(()), dma(()), dma(()), dma(()),
             dma(()), dma(()), dma(()), dma(()), dma(()), dma(()),
         ],

time: 66.2 us -> 63.8 us (0.964)
  Pallas kernels: 61.9 us -> 59.5 us
    pallas_call x1, Pallas kernels: 61.9 us -> 59.5 us  [shards(): pl.pallas_call(kernel, out_shape=(jax.ShapeDtypeStruct((64, 256), bf16),...]
where the time goes in v3:
time: 63.8 us; the launch traced here: 63.5 us
  Pallas kernels  59.5 us (93%)
  local copies, waits for them, and re-layouts  2.75 us (4%)
  between operations  1.29 us (2%)
    pallas_call x1, Pallas kernels, shards(): pl.pallas_call(kernel, out_shape=(jax.ShapeDtypeStruct((64, 256), bf16),...  59.5 us
    unnamed x2, local copies, waits for them, and re-layouts  2.75 us

profile of v3, /device:TPU:8, one launch (start us, length us, event | category | flops | bytes accessed | tf_op | source)
XLA Modules:
  0.0 63.5 jit_solution(6979788942738557921)
XLA Ops:
  1.3 59.5 %layer.1 = (bf16[64,256]{1,0:T(8,128)(2,1)}, f32[32,256]{1,0:T(8,128)}) custom-call(s32[128]{0:T(128)} %rows_hbm.1, s32[128]{0:T(128)} %cols_hbm.1, s32[1]{0:T(128)S(6)} %copy.11.count_hbm, bf16[32,256]{1,0:T(8,128)(2,1)} %feat_hbm.1, bf16[128,128,128]{2,1,0:T(8,128)(2,1)} %tv_hbm.1, bf16[128,256]{1,0:T(8,128)(2,1)} %weight_hbm.1, bf16[64,256]{1,0:T(8,128)(2,1)} %bitcast.2), custom_call_target="tpu_custom_call" | custom-call | tf_op jit(solution)/shard_map/layer/pallas_call | solution.py:293
  60.8 1.4 %copy.12 = bf16[256,64]{0,1:T(8,128)(2,1)} copy(bf16[256,64]{0,1:T(8,128)(2,1)} %bitcast.3) | data formatting | bytes 65536
  62.1 1.4 %copy.13 = f32[32,256]{1,0:T(8,128)} copy(f32[32,256]{1,0:T(8,128)} %get-tuple-element.9) | data formatting | bytes 65536

commit v4 on v3

--- a/solution.py
+++ b/solution.py
@@ -14,7 +14,7 @@
 PER = GROUP // SUB
 TILE = 128
 SLOTS = 128
-BATCH = 8
+BATCH = 32
 
 
 def mod(a, n):
@@ -134,8 +134,6 @@
             for side in range(2):
                 put(ref, ref, ring_send.at[half, side], two_recv.at[half, side, q],
                     ahead[half][side][1])
-                put(ref, ref, ring_send.at[half, side], rest_recv.at[half, side, 0],
-                    ahead[half][side][0])
 
     def pass_piece(q):
         for half in range(2):
@@ -164,6 +162,12 @@
     @pl.loop(SUB - LEAD, SUB)
     def _(q):
         pass_piece(q)
+
+    for half in range(2):
+        for side in range(2):
+            ref = piece(half, mine[half], 0, GROUP)
+            put(ref, ref, ring_send.at[half, side], rest_recv.at[half, side, 0],
+                ahead[half][side][0])
 
     for c in ins[3:]:
         c.wait()
@@ -293,8 +297,8 @@
     hidden_t, d_weight = pl.pallas_call(
         kernel,
         out_shape=(
-            jax.ShapeDtypeStruct((64, 256), bf16),
-            jax.ShapeDtypeStruct((32, 256), f32),
+            pltpu.VMEM((64, 256), bf16),
+            pltpu.VMEM((32, 256), f32),
         ),
         in_specs=[hbm] * 7,
         out_specs=(vmem, vmem),

time: 63.8 us -> 59.2 us (0.928)
  Pallas kernels: 59.5 us -> 56.6 us
  local copies, waits for them, and re-layouts: 2.75 us -> 1.23 us
    pallas_call x1, Pallas kernels: 59.5 us -> 56.6 us  [shards(): pl.pallas_call(kernel, out_shape=(pltpu.VMEM((64, 256), bf16), pltpu.VMEM...]
    unnamed x2, local copies, waits for them, and re-layouts: 2.75 us -> 1.23 us
where the time goes in v4:
time: 59.2 us; the launch traced here: 59.1 us
  Pallas kernels  56.6 us (96%)
  between operations  1.29 us (2%)
  local copies, waits for them, and re-layouts  1.23 us (2%)
    pallas_call x1, Pallas kernels, shards(): pl.pallas_call(kernel, out_shape=(pltpu.VMEM((64, 256), bf16), pltpu.VMEM...  56.6 us
    unnamed x2, local copies, waits for them, and re-layouts  1.23 us

profile of v4, /device:TPU:8, one launch (start us, length us, event | category | flops | bytes accessed | tf_op | source)
XLA Modules:
  0.0 59.1 jit_solution(3827898241874424504)
XLA Ops:
  1.3 56.6 %layer.1 = (bf16[64,256]{1,0:T(8,128)(2,1)S(1)}, f32[32,256]{1,0:T(8,128)S(1)}) custom-call(s32[128]{0:T(128)} %rows_hbm.1, s32[128]{0:T(128)} %cols_hbm.1, s32[1]{0:T(128)S(6)} %copy.13.count_hbm, bf16[32,256]{1,0:T(8,128)(2,1)} %feat_hbm.1, bf16[128,128,128]{2,1,0:T(8,128)(2,1)} %tv_hbm.1, bf16[128,256]{1,0:T(8,128)(2,1)} %weight_hbm.1, ...), custom_call_target="tpu_custom_call" | custom-call | tf_op jit(solution)/shard_map/layer/pallas_call | solution.py:297
  57.9 0.6 %copy.11 = bf16[256,64]{0,1:T(8,128)(2,1)} copy(bf16[256,64]{0,1:T(8,128)(2,1)S(1)} %bitcast.2) | data formatting | bytes 65536
  58.5 0.6 %copy.12 = f32[32,256]{1,0:T(8,128)} copy(f32[32,256]{1,0:T(8,128)S(1)} %get-tuple-element.7) | data formatting | bytes 65536

commit v5 on v4

--- a/solution.py
+++ b/solution.py
@@ -10,7 +10,7 @@
 RING = 8
 GROUP = 16
 SUB = 8
-LEAD = 5
+LEAD = 7
 PER = GROUP // SUB
 TILE = 128
 SLOTS = 128
@@ -109,6 +109,10 @@
     def _(k):
         for half in range(2):
             spread(half, far_first(k), 1)
+
+    @pl.loop(0, RING - 1)
+    def _(k):
+        for half in range(2):
             spread(half, far_first(k), 0)
 
     ins[2].wait()
@@ -274,10 +278,6 @@
     def _(k):
         put(end_buf.at[y], end_buf.at[y], end_send, end_recv, peer(0, far_first(k)))
 
-    waits(end_buf.at[seven], end_recv)
-    for j in range(8):
-        dw_ref[8 * (j // 2):8 * (j // 2) + 8, TILE * (j % 2):TILE * (j % 2) + TILE] = end_buf[j]
-
     for half in range(2):
         waits(table.at[pl.ds(0, GROUP - 1)], first_send.at[half])
         for side in range(2):
@@ -286,6 +286,11 @@
     waits(agg_all.at[three], agg_send)
     waits(rs_buf.at[seven], rs_send)
     waits(mid_buf.at[fifteen], mid_send)
+
+    waits(end_buf.at[seven], end_recv)
+    for j in range(8):
+        dw_ref[8 * (j // 2):8 * (j // 2) + 8, TILE * (j % 2):TILE * (j % 2) + TILE] = end_buf[j]
+
     waits(end_buf.at[seven], end_send)
 
 

time: 59.2 us -> 58.5 us (0.988)
  Pallas kernels: 56.6 us -> 55.9 us
    pallas_call x1, Pallas kernels: 56.6 us -> 55.9 us  [shards(): pl.pallas_call(kernel, out_shape=(pltpu.VMEM((64, 256), bf16), pltpu.VMEM...]
where the time goes in v5:
time: 58.5 us; the launch traced here: 58.4 us
  Pallas kernels  55.9 us (96%)
  between operations  1.29 us (2%)
  local copies, waits for them, and re-layouts  1.23 us (2%)
    pallas_call x1, Pallas kernels, shards(): pl.pallas_call(kernel, out_shape=(pltpu.VMEM((64, 256), bf16), pltpu.VMEM...  55.9 us
    unnamed x2, local copies, waits for them, and re-layouts  1.23 us

profile of v5, /device:TPU:8, one launch (start us, length us, event | category | flops | bytes accessed | tf_op | source)
XLA Modules:
  0.0 58.4 jit_solution(3761697889527923643)
XLA Ops:
  1.3 55.9 %layer.1 = (bf16[64,256]{1,0:T(8,128)(2,1)S(1)}, f32[32,256]{1,0:T(8,128)S(1)}) custom-call(s32[128]{0:T(128)} %rows_hbm.1, s32[128]{0:T(128)} %cols_hbm.1, s32[1]{0:T(128)S(6)} %copy.13.count_hbm, bf16[32,256]{1,0:T(8,128)(2,1)} %feat_hbm.1, bf16[128,128,128]{2,1,0:T(8,128)(2,1)} %tv_hbm.1, bf16[128,256]{1,0:T(8,128)(2,1)} %weight_hbm.1, ...), custom_call_target="tpu_custom_call" | custom-call | tf_op jit(solution)/shard_map/layer/pallas_call | solution.py:302
  57.2 0.6 %copy.11 = bf16[256,64]{0,1:T(8,128)(2,1)} copy(bf16[256,64]{0,1:T(8,128)(2,1)S(1)} %bitcast.2) | data formatting | bytes 65536
  57.8 0.6 %copy.12 = f32[32,256]{1,0:T(8,128)} copy(f32[32,256]{1,0:T(8,128)S(1)} %get-tuple-element.7) | data formatting | bytes 65536

commit v6 on v5

--- a/solution.py
+++ b/solution.py
@@ -27,6 +27,11 @@
 
 def far_first(k):
     return RING // 2 + lax.div(k + 1, jnp.int32(2)) * (1 - 2 * mod(k, 2))
+
+
+def near_first(k):
+    near = lax.div(k, jnp.int32(2)) + 1
+    return jnp.where(mod(k, 2) == 0, near, RING - near)
 
 
 def kernel(
@@ -113,7 +118,7 @@
     @pl.loop(0, RING - 1)
     def _(k):
         for half in range(2):
-            spread(half, far_first(k), 0)
+            spread(half, near_first(k), 0)
 
     ins[2].wait()
 
@@ -211,10 +216,10 @@
         lhs = jnp.concatenate(picks, axis=1)
         rhs = jnp.concatenate([tv[b * BATCH + j] for j in range(BATCH)], axis=1)
         return acc + lax.dot_general(
-            lhs, rhs, (((1,), (1,)), ((), ())), preferred_element_type=jnp.float32
+            rhs, lhs, (((1,), (1,)), ((), ())), preferred_element_type=jnp.float32
         )
 
-    acc = lax.fori_loop(0, SLOTS // BATCH, batch, jnp.zeros((64, TILE), jnp.float32))
+    acc = lax.fori_loop(0, SLOTS // BATCH, batch, jnp.zeros((TILE, 64), jnp.float32)).T
     agg = jnp.concatenate([acc[:32], acc[32:]], axis=1).astype(jnp.bfloat16)
     agg_all[rep] = agg
 

time: 58.5 us -> 58.4 us (level)
  no operation moved by 1% of the time
where the time goes in v6:
time: 58.4 us; the launch traced here: 58.3 us
  Pallas kernels  55.8 us (96%)
  between operations  1.29 us (2%)
  local copies, waits for them, and re-layouts  1.23 us (2%)
    pallas_call x1, Pallas kernels, shards(): pl.pallas_call(kernel, out_shape=(pltpu.VMEM((64, 256), bf16), pltpu.VMEM...  55.8 us
    unnamed x2, local copies, waits for them, and re-layouts  1.23 us

profile of v6, /device:TPU:8, one launch (start us, length us, event | category | flops | bytes accessed | tf_op | source)
XLA Modules:
  0.0 58.3 jit_solution(4762784805997141305)
XLA Ops:
  1.3 55.8 %layer.1 = (bf16[64,256]{1,0:T(8,128)(2,1)S(1)}, f32[32,256]{1,0:T(8,128)S(1)}) custom-call(s32[128]{0:T(128)} %rows_hbm.1, s32[128]{0:T(128)} %cols_hbm.1, s32[1]{0:T(128)S(6)} %copy.13.count_hbm, bf16[32,256]{1,0:T(8,128)(2,1)} %feat_hbm.1, bf16[128,128,128]{2,1,0:T(8,128)(2,1)} %tv_hbm.1, bf16[128,256]{1,0:T(8,128)(2,1)} %weight_hbm.1, ...), custom_call_target="tpu_custom_call" | custom-call | tf_op jit(solution)/shard_map/layer/pallas_call | solution.py:307
  57.0 0.6 %copy.11 = bf16[256,64]{0,1:T(8,128)(2,1)} copy(bf16[256,64]{0,1:T(8,128)(2,1)S(1)} %bitcast.2) | data formatting | bytes 65536
  57.7 0.6 %copy.12 = f32[32,256]{1,0:T(8,128)} copy(f32[32,256]{1,0:T(8,128)S(1)} %get-tuple-element.7) | data formatting | bytes 65536
